TPU v7x, 32 devices: a whole 2x2x4 slice. The times are simulated.
32 devices in a mesh: grp: 2 (over x), node: 16 (over z, y, core).
Axes of the slice: x: 2, y: 2, z: 4, core: 2. Of those that a mesh axis runs over, the one named last changes fastest.
Arguments:
- nodes: bfloat16 [128, 2, 1024, 1024], P('grp', None, 'node'), parts along dimension 0, may hold values from -0.34960938 to 0.34960938
- pair_nodes: int32 [16, 2], replicated, may hold values from 0 to 63
- prod_left: int32 [16], replicated, may hold values from 0 to 15, as said below
- prod_right: int32 [16], replicated, may hold values from 0 to 15, each once
- prod_flag: int32 [16], replicated, may hold values from 0 to 1
- prod_diag: int32 [16], replicated, may hold values from 0 to 7, as said below
Outputs:
- diagrams: bfloat16 [16, 2, 1024, 1024], P('grp', None, 'node'), parts along dimension 0
There are 2 independent parts, one for each index of `grp`. A program takes and returns all parts, laid end to end along the dimension named above; an argument that names none is the same for every part. Nothing has to cross between parts.
Inputs may be any that keep to these rules, and one draw needn't show every extreme that they name: `prod_left`: exactly 8 distinct pairs are left operands, each of exactly two products. `prod_diag`: every diagram receives exactly two products.
All inputs are finite; a program needn't handle non-finite values.
Results may differ from a plain program's by a relative error of at most 0.0065.
Values may be sent and summed in bfloat16 or wider, within the bound.
No kernel may reach another device: no remote copies, remote signals or barrier semaphores. Data moves between devices by JAX's collectives and lax.ppermute only.
A program may use at most 128 MiB of HBM per device.

v0:
```python
import jax
import jax.numpy as jnp
from jax import lax
from jax.sharding import PartitionSpec as P


def complex_product(left_re, left_im, right_re, right_im):
    real_part = jnp.einsum(
        "lij,ljk->lik", left_re, right_re, preferred_element_type=jnp.float32
    ) - jnp.einsum("lij,ljk->lik", left_im, right_im, preferred_element_type=jnp.float32)
    imag_part = jnp.einsum(
        "lij,ljk->lik", left_re, right_im, preferred_element_type=jnp.float32
    ) + jnp.einsum("lij,ljk->lik", left_im, right_re, preferred_element_type=jnp.float32)
    return jnp.stack([real_part, imag_part], axis=1).astype(jnp.bfloat16)


def adjoint_where(left_re, left_im, my_flags):
    flipped = my_flags[:, None, None] == 1
    return (
        jnp.where(flipped, jnp.swapaxes(left_re, 1, 2), left_re),
        jnp.where(flipped, -jnp.swapaxes(left_im, 1, 2), left_im),
    )


def local(nodes, pair_nodes, prod_left, prod_right, prod_flag, prod_diag):
    position = lax.axis_index("node")
    pairs_all = pair_nodes.shape[0]
    prods_all = prod_left.shape[0]
    diags_all = prods_all // 2
    ordered_nodes = jnp.take(pair_nodes, prod_right, axis=0)
    left_nodes = jnp.take(nodes, ordered_nodes[:, 0], axis=0)
    right_nodes = jnp.take(nodes, ordered_nodes[:, 1], axis=0)
    outgoing = jnp.stack([left_nodes, right_nodes], axis=1)
    assembled = lax.all_to_all(outgoing, "node", split_axis=0, concat_axis=3, tiled=True)
    paired = complex_product(
        assembled[:, 0, 0], assembled[:, 0, 1], assembled[:, 1, 0], assembled[:, 1, 1]
    )
    panels = lax.all_to_all(paired, "node", split_axis=2, concat_axis=0, tiled=True)
    diag_hot = (prod_diag[None, :] == jnp.arange(diags_all, dtype=jnp.int32)[:, None]).astype(
        jnp.int32
    )
    numbers = jnp.arange(pairs_all, dtype=jnp.int32)
    where_pair = jnp.sum(
        (prod_right[None, :] == prod_left[:, None]).astype(jnp.int32) * numbers[None, :], axis=1
    )
    left_sel = jnp.take(panels, where_pair, axis=0)
    left_full = lax.all_to_all(left_sel, "node", split_axis=0, concat_axis=2, tiled=True)
    local_count = left_full.shape[0]
    my_flags = lax.dynamic_slice_in_dim(prod_flag, position * local_count, local_count)
    left_re, left_im = adjoint_where(left_full[:, 0], left_full[:, 1], my_flags)
    results = complex_product(left_re, left_im, paired[:, 0], paired[:, 1])
    result_panels = lax.all_to_all(results, "node", split_axis=2, concat_axis=0, tiled=True)
    rows_all = result_panels.shape[0]
    summed = jnp.dot(
        diag_hot.astype(jnp.bfloat16),
        result_panels.reshape(rows_all, -1),
        preferred_element_type=jnp.float32,
    )
    return summed.reshape(diags_all, 2, result_panels.shape[2], result_panels.shape[3]).astype(
        jnp.bfloat16
    )


def solution(mesh):
    placed = (P("grp", None, "node", None), P(), P(), P(), P(), P())
    return jax.shard_map(
        local, mesh=mesh, in_specs=placed, out_specs=P("grp", None, "node", None), check_vma=False
    )
```

profile of v0, /device:TPU:10, one launch (start us, length us, event | category | flops | bytes accessed | tf_op | source)
XLA Modules:
  0.0 623.5 jit_solution(2190018857934509209)
XLA Ops:
  3.0 8.6 %gather_fusion.2 = bf16[16,2,64,1024]{3,2,1,0:T(8,128)(2,1)} fusion(bf16[64,2,64,1024]{3,2,1,0:T(8,128)(2,1)} %param.8, s32[1024]{0:T(1024)S(1)} %pad_clamp_fusion.2), kind=kCustom, calls=%fused_computation.clone | custom fusion | bytes 8388672 | tf_op jit(solution)/shard_map/jit(_take)/gather | solution.py:31
  11.5 8.5 %gather_fusion.3 = bf16[16,2,64,1024]{3,2,1,0:T(8,128)(2,1)} fusion(bf16[64,2,64,1024]{3,2,1,0:T(8,128)(2,1)} %param.8, s32[1024]{0:T(1024)S(1)} %pad_clamp_fusion.1), kind=kCustom, calls=%fused_computation.1.clone | custom fusion | bytes 8388672 | tf_op jit(solution)/shard_map/jit(_take)/gather | solution.py:32
  20.0 2.8 select_bitcast_fusion.1
  23.5 2.4 select_bitcast_fusion
  25.9 6.2 pad_maximum_fusion
  32.1 8.4 %copy.51 = bf16[16,2,2,64,1024]{4,3,2,1,0:T(8,128)(2,1)} copy(bf16[16,2,2,64,1024]{4,3,2,0,1:T(8,128)(2,1)} %pad_maximum_fusion) | data formatting | bytes 16777216 | tf_op jit(solution)/shard_map/stack | solution.py:33
  40.5 188.6 %all_to_all.69 = bf16[16,2,2,64,1024]{4,3,2,1,0:T(8,128)(2,1)} all-to-all(bf16[16,2,2,64,1024]{4,3,2,1,0:T(8,128)(2,1)} %copy.51), channel_id=1, replica_groups=mesh['grp'=2,'node'=16] {'node'}, dimensions={0} | all-to-all | bytes 16777216 | tf_op jit(solution)/shard_map/all_to_all | solution.py:34
  229.1 8.4 %copy.52 = bf16[16,2,2,64,1024]{4,3,0,2,1:T(8,128)(2,1)} copy(bf16[16,2,2,64,1024]{4,3,2,1,0:T(8,128)(2,1)} %all_to_all.69) | data formatting | bytes 16777216 | tf_op jit(solution)/shard_map/all_to_all | solution.py:34
  237.5 4.7 fusion.15
  246.9 2.3 subtract_convert_fusion.1
  250.9 6.4 %copy.53 = bf16[1,2,1024,1024]{3,1,0,2:T(2,128)(2,1)} copy(bf16[1,2,1024,1024]{3,2,1,0:T(8,128)(2,1)S(1)} %pad_maximum_fusion.1) | data formatting | bytes 8388608 | tf_op jit(solution)/shard_map/stack | solution.py:14
  257.4 5.8 all-to-all-start.1
  263.4 90.6 %all-to-all-done.1 = bf16[1,2,1024,1024]{3,1,0,2:T(2,128)(2,1)} async-done(((bf16[1,2,1024,1024]{3,1,0,2:T(2,128)(2,1)}), bf16[1,2,1024,1024]{3,1,0,2:T(2,128)(2,1)}, u32[]{:S(2)}, u32[]{:S(2)}) %all-to-all-start.1) | async-done | bytes 4194336 | tf_op jit(solution)/shard_map/all_to_all | solution.py:38
  354.0 5.5 copy.73
  359.5 5.0 gather_fusion.1
  364.5 4.6 broadcast_select_fusion
  369.1 6.7 %all-to-all-start.2 = ((bf16[16,2,64,1024]{3,2,1,0:T(8,128)(2,1)}), bf16[16,2,64,1024]{3,2,1,0:T(8,128)(2,1)}, u32[]{:S(2)}, u32[]{:S(2)}) async-start(bf16[16,2,64,1024]{3,2,1,0:T(8,128)(2,1)} %broadcast_select_fusion), calls=%async_computation.2 | async-start | bytes 8388608 | tf_op jit(solution)/shard_map/all_to_all | solution.py:47
  377.2 89.5 %all-to-all-done.2 = bf16[16,2,64,1024]{3,2,1,0:T(8,128)(2,1)} async-done(((bf16[16,2,64,1024]{3,2,1,0:T(8,128)(2,1)}), bf16[16,2,64,1024]{3,2,1,0:T(8,128)(2,1)}, u32[]{:S(2)}, u32[]{:S(2)}) %all-to-all-start.2) | async-done | bytes 4194336 | tf_op jit(solution)/shard_map/all_to_all | solution.py:47
  466.6 2.6 copy.56
  471.8 3.9 copy.58
  475.8 7.3 %fusion.4 = f32[1024,1024]{1,0:T(8,128)} fusion(bf16[1024,1024]{1,0:T(8,128)(2,1)} %copy-done.7, bf16[1,1024,1024]{1,2,0:T(8,128)(2,1)} %copy.58, pred[]{:T(512)} %bitcast.2, bf16[1,2,1024,1024]{3,2,1,0:T(8,128)(2,1)} %bitcast.111), kind=kOutput, calls=%fused_computation.25 | convolution fusion | flops 2149580800 | bytes 10486272 | tf_op jit(solution)/shard_map/lij,ljk->lik/dot_general | solution.py:13
  483.1 4.3 fusion.6
  487.4 2.8 copy.57
  490.2 6.6 %fusion.3 = bf16[1,1,1024,1024]{3,2,1,0:T(8,128)(2,1)S(1)} fusion(f32[1024,1024]{1,0:T(8,128)} %fusion.4, bf16[1024,1024]{1,0:T(8,128)(2,1)} %copy-done.9, bf16[1,1024,1024]{2,1,0:T(8,128)(2,1)} %copy.57, pred[]{:T(512)} %bitcast.2, bf16[1,2,1024,1024]{3,2,1,0:T(8,128)(2,1)} %bitcast.112), kind=kOutput, calls=%fused_computation.19 | convolution fusion | flops 2150629376 | bytes 12583424 | tf_op jit(solution)/shard_map/lij,ljk->lik/dot_general | solution.py:11
  497.9 2.4 fusion.2
  500.7 6.3 %copy.59 = bf16[1,2,1024,1024]{3,1,0,2:T(2,128)(2,1)} copy(bf16[1,2,1024,1024]{3,2,1,0:T(8,128)(2,1)S(1)} %pad_maximum_fusion.2) | data formatting | bytes 8388608 | tf_op jit(solution)/shard_map/stack | solution.py:14
  507.0 98.6 %all_to_all.70 = bf16[1,2,1024,1024]{3,1,0,2:T(2,128)(2,1)S(1)} all-to-all(bf16[1,2,1024,1024]{3,1,0,2:T(2,128)(2,1)} %copy.59), channel_id=1, replica_groups=mesh['grp'=2,'node'=16] {'node'}, dimensions={2} | all-to-all | bytes 8388608 | tf_op jit(solution)/shard_map/all_to_all | solution.py:52
  605.6 3.3 copy.74
  608.9 4.8 reshape.182
  613.8 4.5 copy.66
  618.3 2.4 fusion.12
  620.7 2.5 copy.62
  (53 shorter events, 14.9 us)
Async XLA Ops:
  20.0 3.4 copy-start.3
  237.5 4.7 copy-start.4
  246.9 2.4 copy-start.9
  249.2 1.3 copy-start.7
  257.4 5.8 copy-start.12
  257.4 5.8 copy-start.13
  257.4 96.6 %all-to-all-start.1 = ((bf16[1,2,1024,1024]{3,1,0,2:T(2,128)(2,1)}), bf16[1,2,1024,1024]{3,1,0,2:T(2,128)(2,1)}, u32[]{:S(2)}, u32[]{:S(2)}) async-start(bf16[1,2,1024,1024]{3,1,0,2:T(2,128)(2,1)} %copy.53), calls=%async_computation.1 | async-start | bytes 8388608 | tf_op jit(solution)/shard_map/all_to_all | solution.py:38
  369.1 6.7 %copy-start.14 = (s32[16]{0:T(128)S(1)}, s32[16]{0:T(128)}, u32[]{:S(2)}) copy-start(s32[16]{0:T(128)} %param.12) | copy-start | bytes 196
  369.1 97.5 %all-to-all-start.2 = ((bf16[16,2,64,1024]{3,2,1,0:T(8,128)(2,1)}), bf16[16,2,64,1024]{3,2,1,0:T(8,128)(2,1)}, u32[]{:S(2)}, u32[]{:S(2)}) async-start(bf16[16,2,64,1024]{3,2,1,0:T(8,128)(2,1)} %broadcast_select_fusion), calls=%async_computation.2 | async-start | bytes 8388608 | tf_op jit(solution)/shard_map/all_to_all | solution.py:47
  469.3 2.6 copy-start
  475.8 7.3 %copy-start.1 = (bf16[1,2,16,64,1024]{4,3,2,1,0:T(8,128)(2,1)S(1)}, bf16[1,2,16,64,1024]{4,3,2,1,0:T(8,128)(2,1)}, u32[]{:S(2)}) copy-start(bf16[1,2,16,64,1024]{4,3,2,1,0:T(8,128)(2,1)} %copy-done) | copy-start | bytes 12582916
  475.8 7.3 %copy-start.6 = (bf16[1,1024,1024]{1,2,0:T(8,128)(2,1)S(1)}, bf16[1,1024,1024]{1,2,0:T(8,128)(2,1)}, u32[]{:S(2)}) copy-start(bf16[1,1024,1024]{1,2,0:T(8,128)(2,1)} %copy.58) | copy-start | bytes 6291460
  475.8 7.3 %copy-start.10 = (bf16[1024,1024]{1,0:T(8,128)(2,1)S(1)}, bf16[1024,1024]{1,0:T(8,128)(2,1)}, u32[]{:S(2)}) copy-start(bf16[1024,1024]{1,0:T(8,128)(2,1)} %copy-done.9) | copy-start | bytes 6291460
  490.2 6.6 %copy-start.2 = (bf16[1,2,16,64,1024]{4,3,2,1,0:T(8,128)(2,1)S(1)}, bf16[1,2,16,64,1024]{4,3,2,1,0:T(8,128)(2,1)}, u32[]{:S(2)}) copy-start(bf16[1,2,16,64,1024]{4,3,2,1,0:T(8,128)(2,1)} %copy-done) | copy-start | bytes 12582916
  490.2 6.6 %copy-start.5 = (bf16[1,1024,1024]{2,1,0:T(8,128)(2,1)S(1)}, bf16[1,1024,1024]{2,1,0:T(8,128)(2,1)}, u32[]{:S(2)}) copy-start(bf16[1,1024,1024]{2,1,0:T(8,128)(2,1)} %copy.57) | copy-start | bytes 6291460
  490.2 6.6 %copy-start.8 = (bf16[1024,1024]{1,0:T(8,128)(2,1)S(1)}, bf16[1024,1024]{1,0:T(8,128)(2,1)}, u32[]{:S(2)}) copy-start(bf16[1024,1024]{1,0:T(8,128)(2,1)} %copy-done.7) | copy-start | bytes 6291460
  490.2 7.7 %copy-start.15 = (f32[1024,1024]{1,0:T(8,128)S(1)}, f32[1024,1024]{1,0:T(8,128)}, u32[]{:S(2)}) copy-start(f32[1024,1024]{1,0:T(8,128)} %fusion.6) | copy-start | bytes 12582916
  613.8 4.5 copy-start.11
where the time goes:
time: 629 us; the launch traced here: 623 us
  blocking collectives  287 us (46%)
  waiting for transfers between devices  180 us (29%)
  local copies, waits for them, and re-layouts  89.5 us (14%)
  matrix products  34.6 us (6%)
  other arithmetic  18.4 us (3%)
  starting transfers between devices  12.5 us (2%)
    all_to_all x1, blocking collectives, local(): lax.all_to_all(outgoing, 'node', split_axis=0, concat_axis=3, tiled=True)  189 us
    all_to_all x1, blocking collectives, local(): lax.all_to_all(results, 'node', split_axis=2, concat_axis=0, tiled=True)  98.6 us
    all_to_all x1, waiting for transfers between devices, local(): lax.all_to_all(paired, 'node', split_axis=2, concat_axis=0, tiled=True)  90.6 us
    all_to_all x1, waiting for transfers between devices, local(): lax.all_to_all(left_sel, 'node', split_axis=0, concat_axis=2, tiled=True)  89.5 us
    another operation x2, local copies, waits for them, and re-layouts, complex_product(): return jnp.stack([real_part, imag_part], axis=1).astype(jnp.bfloat16)  12.7 us
  transfers between devices with their start and end apart: 2, of which 2 were waited for; matrix products, arithmetic and copies ran while one was open for 0% of the time, Pallas kernels for 0%

commit v1 on v0

v1 whole, which is shorter than its diff:
```python
import functools

import jax
import jax.numpy as jnp
from jax import lax
from jax.experimental import pallas as pl
from jax.experimental.pallas import tpu as pltpu
from jax.sharding import PartitionSpec as P

PARTS = 2
VMEM_BYTES = 48 * 1024 * 1024
SMEM = pl.BlockSpec(memory_space=pltpu.SMEM)
HBM = pl.BlockSpec(memory_space=pl.ANY)
VMEM = pl.BlockSpec(memory_space=pltpu.VMEM)


def params():
    return pltpu.CompilerParams(vmem_limit_bytes=VMEM_BYTES)


def route_kernel(prods, pair_nodes, prod_left, prod_right, prod_flag, prod_diag, table):
    half = prods // 2

    def clear(d, carry):
        table[5, d] = -1
        return carry

    lax.fori_loop(0, prods, clear, 0)

    def rank(k, carry):
        mine = prod_left[k]

        def count(j, total):
            other = prod_left[j]
            before = jnp.logical_or(other < mine, jnp.logical_and(other == mine, j < k))
            return total + before.astype(jnp.int32)

        place = lax.fori_loop(0, prods, count, 0, unroll=True)
        right = prod_right[k]
        table[0, place] = pair_nodes[mine, lax.rem(place, 2)]
        table[1, place] = pair_nodes[right, 0]
        table[2, place] = pair_nodes[right, 1]
        table[3, place] = prod_flag[k]
        table[4, place] = prod_diag[k]
        return carry

    lax.fori_loop(0, prods, rank, 0)

    def diagram(place, carry):
        d = table[4, place]
        second = (table[5, d] >= 0).astype(jnp.int32)
        table[5, d + second * half] = place
        return carry

    lax.fori_loop(0, prods, diagram, 0)


def route(pair_nodes, prod_left, prod_right, prod_flag, prod_diag):
    prods = prod_left.shape[0]
    return pl.pallas_call(
        functools.partial(route_kernel, prods),
        out_shape=jax.ShapeDtypeStruct((8, prods), jnp.int32),
        in_specs=[SMEM] * 5,
        out_specs=SMEM,
        name="route",
    )(pair_nodes, prod_left, prod_right, prod_flag, prod_diag)


def pick_kernel(table, node, out):
    out[...] = node[...]


def pick(table, nodes, row, part, width):
    count = table.shape[1]
    block = (1, nodes.shape[1], nodes.shape[2], width)
    return pl.pallas_call(
        pick_kernel,
        out_shape=jax.ShapeDtypeStruct((count,) + block[1:], nodes.dtype),
        grid_spec=pltpu.PrefetchScalarGridSpec(
            num_scalar_prefetch=1,
            grid=(count,),
            in_specs=[pl.BlockSpec(block, lambda t, table: (table[row, t], 0, 0, part))],
            out_specs=pl.BlockSpec(block, lambda t, table: (t, 0, 0, 0)),
        ),
        cost_estimate=pl.CostEstimate(
            flops=0, transcendentals=0, bytes_accessed=4 * count * block[1] * block[2] * width
        ),
        name="pick",
    )(table, nodes)


def dot(a, b):
    return jnp.dot(a, b, preferred_element_type=jnp.float32)


def left_kernel(table, place, own, other, out, left, right, sems):
    order = left.shape[2] * left.shape[0]
    core = lax.rem(place[0], 2)
    flag = table[3, place[0]]

    def load(first, second):
        one = pltpu.make_async_copy(first, left, sems.at[0])
        two = pltpu.make_async_copy(second, right, sems.at[1])
        one.start()
        two.start()
        one.wait()
        two.wait()

    @pl.when(core == 0)
    def _():
        load(own, other)

    @pl.when(core == 1)
    def _():
        load(other, own)

    b_re = right[:, 0].reshape(order, order)
    b_im = right[:, 1].reshape(order, order)
    step = order // 4
    per = left.shape[0] // 4
    for block in range(4):
        a_re = left[block * per : (block + 1) * per, 0].reshape(step, order)
        a_im = left[block * per : (block + 1) * per, 1].reshape(step, order)
        re = (dot(a_re, b_re) - dot(a_im, b_im)).astype(out.dtype)
        im = (dot(a_re, b_im) + dot(a_im, b_re)).astype(out.dtype)

        @pl.when(flag == 0)
        def _():
            out[0, block * step : (block + 1) * step, :] = re
            out[1, block * step : (block + 1) * step, :] = im

        @pl.when(flag == 1)
        def _():
            out[0, :, block * step : (block + 1) * step] = re.T
            out[1, :, block * step : (block + 1) * step] = -im.T


def left_pair(table, place, own, other):
    order = own.shape[3]
    return pl.pallas_call(
        left_kernel,
        out_shape=jax.ShapeDtypeStruct((2, order, order), own.dtype),
        in_specs=[SMEM, SMEM, HBM, HBM],
        out_specs=VMEM,
        scratch_shapes=[
            pltpu.VMEM(own.shape, own.dtype),
            pltpu.VMEM(own.shape, own.dtype),
            pltpu.SemaphoreType.DMA((2,)),
        ],
        compiler_params=params(),
        cost_estimate=pl.CostEstimate(
            flops=8 * order**3, transcendentals=0, bytes_accessed=12 * order * order
        ),
        name="left_pair",
    )(table, place, own, other)


def product_kernel(left, right, out):
    order = left.shape[2]
    width = right.shape[3]
    b_re = right[:, 0].reshape(order, width)
    b_im = right[:, 1].reshape(order, width)
    step = order // 4
    panels = len(out.shape) == 4
    for block in range(4):
        rows = slice(block * step, (block + 1) * step)
        a_re = left[0, rows, :]
        a_im = left[1, rows, :]
        re = (dot(a_re, b_re) - dot(a_im, b_im)).astype(out.dtype)
        im = (dot(a_re, b_im) + dot(a_im, b_re)).astype(out.dtype)
        if panels:
            per = out.shape[0] // 4
            place = slice(block * per, (block + 1) * per)
            out[place, 0] = re.reshape(per, out.shape[2], width)
            out[place, 1] = im.reshape(per, out.shape[2], width)
        else:
            out[0, rows, :] = re
            out[1, rows, :] = im


def product(left, right, panels):
    order = left.shape[2]
    width = right.shape[3]
    shape = right.shape if panels else (2, order, width)
    return pl.pallas_call(
        product_kernel,
        out_shape=jax.ShapeDtypeStruct(shape, left.dtype),
        in_specs=[VMEM, VMEM],
        out_specs=VMEM,
        compiler_params=params(),
        cost_estimate=pl.CostEstimate(
            flops=8 * order * order * width,
            transcendentals=0,
            bytes_accessed=4 * (order * order + 2 * order * width),
        ),
        name="product",
    )(left, right)


def diagrams_kernel(table, *refs):
    parts, out = refs[:-1], refs[-1]
    width = parts[0].shape[3]
    d = pl.program_id(0)
    half = table.shape[1] // 2
    one, two = table[5, d], table[5, d + half]
    for j, part in enumerate(parts):
        total = part[one].astype(jnp.float32) + part[two].astype(jnp.float32)
        out[0, :, :, j * width : (j + 1) * width] = total.astype(out.dtype)


def diagrams_of(table, parts):
    count, two, rows, width = parts[0].shape
    whole = width * len(parts)
    return pl.pallas_call(
        diagrams_kernel,
        out_shape=jax.ShapeDtypeStruct((count // 2, two, rows, whole), parts[0].dtype),
        grid=(count // 2,),
        in_specs=[SMEM] + [VMEM] * len(parts),
        out_specs=pl.BlockSpec((1, two, rows, whole), lambda d: (d, 0, 0, 0)),
        compiler_params=params(),
        name="diagrams",
    )(table, *parts)


def exchange(x):
    return lax.all_to_all(x, "node", split_axis=0, concat_axis=0, tiled=True)


def after(x, earlier):
    return lax.optimization_barrier((x, earlier))[0]


def local(size, nodes, pair_nodes, prod_left, prod_right, prod_flag, prod_diag):
    place = lax.axis_index("node").astype(jnp.int32).reshape(1)
    order = nodes.shape[3]
    width = order // PARTS
    table = route(pair_nodes, prod_left, prod_right, prod_flag, prod_diag)
    own = exchange(pick(table, nodes, 0, 0, order))
    other = lax.ppermute(own, "node", [(i, i ^ 1) for i in range(size)])
    middle = exchange(after(pick(table, nodes, 1, 0, order), own))
    left = left_pair(table, place, own, other)
    half = product(left, middle, False)
    arrived = middle
    results = []
    for j in range(PARTS):
        arrived = exchange(after(pick(table, nodes, 2, j, width), arrived))
        results.append(product(half, arrived, True))
    parts = []
    for result in results:
        arrived = exchange(after(result, arrived))
        parts.append(arrived)
    return diagrams_of(table, parts)


def solution(mesh):
    placed = (P("grp", None, "node", None), P(), P(), P(), P(), P())
    return jax.shard_map(
        functools.partial(local, mesh.shape["node"]),
        mesh=mesh,
        in_specs=placed,
        out_specs=P("grp", None, "node", None),
        check_vma=False,
    )
```

time: 629 us -> 427 us (0.68)
  blocking collectives: 287 us -> 53.8 us
  Pallas kernels: 0 us -> 89.3 us
  local copies, waits for them, and re-layouts: 89.5 us -> 7.89 us
  waiting for transfers between devices: 180 us -> 241 us
  matrix products: 34.6 us -> 0 us
  starting transfers between devices: 12.5 us -> 32.6 us
  other arithmetic: 18.4 us -> 0 us
    all_to_all x2 -> x1, blocking collectives: 287 us -> 53.8 us  [exchange(): return lax.all_to_all(x, 'node', split_axis=0, concat_axis=0, tiled=True)]
    pallas_call x0 -> x10, Pallas kernels: none -> 89.3 us  [the longest x4 41.3 us: pick(): pl.pallas_call(pick_kernel, out_shape=jax.ShapeDtypeStruct((count,) + blo...]
    all_to_all x2 -> x5, waiting for transfers between devices: 180 us -> 241 us  [exchange(): return lax.all_to_all(x, 'node', split_axis=0, concat_axis=0, tiled=True)]
    dot_general x9 -> x0, matrix products: 34.6 us -> none  [the longest x2 11.2 us: complex_product(): jnp.einsum('lij,ljk->lik', left_re, right_im, preferred_element_type=jnp....]
    gather x4 -> x0, local copies, waits for them, and re-layouts: 22.6 us -> none  [the longest x1 8.55 us: local(): left_nodes = jnp.take(nodes, ordered_nodes[:, 0], axis=0)]
    another operation x3 -> x0, local copies, waits for them, and re-layouts: 21.1 us -> none  [the longest x2 12.7 us: complex_product(): return jnp.stack([real_part, imag_part], axis=1).astype(jnp.bfloat16)]
    all_to_all x2 -> x5, starting transfers between devices: 12.5 us -> 32.4 us  [exchange(): return lax.all_to_all(x, 'node', split_axis=0, concat_axis=0, tiled=True)]
    all_to_all x4 -> x0, local copies, waits for them, and re-layouts: 19.9 us -> none  [the longest x1 8.42 us: local(): lax.all_to_all(outgoing, 'node', split_axis=0, concat_axis=3, tiled=True)]
  transfers between devices with their start and end apart: 2 -> 6, of which waited for: 2 -> 5; matrix products, arithmetic and copies ran while one was open for 0% -> 0% of each run, Pallas kernels for 0% -> 17%
where the time goes in v1:
time: 427 us; the launch traced here: 424 us
  waiting for transfers between devices  241 us (56%)
  Pallas kernels  89.3 us (21%)
  blocking collectives  53.8 us (13%)
  starting transfers between devices  32.6 us (8%)
  local copies, waits for them, and re-layouts  7.89 us (2%)
    all_to_all x5, waiting for transfers between devices, exchange(): return lax.all_to_all(x, 'node', split_axis=0, concat_axis=0, tiled=True)  241 us
    all_to_all x1, blocking collectives, exchange(): return lax.all_to_all(x, 'node', split_axis=0, concat_axis=0, tiled=True)  53.8 us
    pallas_call x4, Pallas kernels, pick(): pl.pallas_call(pick_kernel, out_shape=jax.ShapeDtypeStruct((count,) + blo...  41.3 us
    all_to_all x5, starting transfers between devices, exchange(): return lax.all_to_all(x, 'node', split_axis=0, concat_axis=0, tiled=True)  32.4 us
    pallas_call x3, Pallas kernels, product(): pl.pallas_call(product_kernel, out_shape=jax.ShapeDtypeStruct(shape, left...  26.5 us
    pallas_call x1, Pallas kernels, left_pair(): pl.pallas_call(left_kernel, out_shape=jax.ShapeDtypeStruct((2, order, ord...  15 us
  transfers between devices with their start and end apart: 6, of which 5 were waited for; matrix products, arithmetic and copies ran while one was open for 0% of the time, Pallas kernels for 17%

profile of v1, /device:TPU:10, one launch (start us, length us, event | category | flops | bytes accessed | tf_op | source)
XLA Modules:
  0.0 424.3 jit_solution(12757928784414931327)
XLA Ops:
  0.0 1.4 copy.7.pair_nodes
  1.4 2.7 route.1.table
  4.1 10.9 %pick.4 = bf16[16,2,64,1024]{3,2,1,0:T(8,128)(2,1)} custom-call(s32[8,16]{1,0:T(8,128)} %route.1.table, bf16[64,2,64,1024]{3,2,1,0:T(8,128)(2,1)} %node.7), custom_call_target="tpu_custom_call" | custom-call | bytes 8388608 | tf_op jit(solution)/shard_map/pick/pallas_call | solution.py:76
  15.0 6.3 %all-to-all-start = ((bf16[16,2,64,1024]{3,2,1,0:T(8,128)(2,1)}), bf16[16,2,64,1024]{3,2,1,0:T(8,128)(2,1)}, u32[]{:S(2)}, u32[]{:S(2)}) async-start(bf16[16,2,64,1024]{3,2,1,0:T(8,128)(2,1)} %pick.4), calls=%async_computation | async-start | bytes 8388608 | tf_op jit(solution)/shard_map/all_to_all | solution.py:226
  21.3 10.9 %pick.5 = bf16[16,2,64,1024]{3,2,1,0:T(8,128)(2,1)} custom-call(s32[8,16]{1,0:T(8,128)} %route.1.table, bf16[64,2,64,1024]{3,2,1,0:T(8,128)(2,1)} %node.7), custom_call_target="tpu_custom_call" | custom-call | bytes 8388608 | tf_op jit(solution)/shard_map/pick/pallas_call | solution.py:76
  32.2 79.9 %all-to-all-done.own = bf16[16,2,64,1024]{3,2,1,0:T(8,128)(2,1)} async-done(((bf16[16,2,64,1024]{3,2,1,0:T(8,128)(2,1)}), bf16[16,2,64,1024]{3,2,1,0:T(8,128)(2,1)}, u32[]{:S(2)}, u32[]{:S(2)}) %all-to-all-start) | async-done | bytes 4194336 | tf_op jit(solution)/shard_map/all_to_all | solution.py:226
  112.1 6.6 %all-to-all-start.1 = ((bf16[16,2,64,1024]{3,2,1,0:T(8,128)(2,1)}), bf16[16,2,64,1024]{3,2,1,0:T(8,128)(2,1)}, u32[]{:S(2)}, u32[]{:S(2)}) async-start(bf16[16,2,64,1024]{3,2,1,0:T(8,128)(2,1)} %pick.5), calls=%async_computation.1 | async-start | bytes 8388608 | tf_op jit(solution)/shard_map/all_to_all | solution.py:226
  118.7 9.7 %pick.6 = bf16[16,2,64,512]{3,2,1,0:T(8,128)(2,1)} custom-call(s32[8,16]{1,0:T(8,128)} %route.1.table, bf16[64,2,64,1024]{3,2,1,0:T(8,128)(2,1)} %node.7), custom_call_target="tpu_custom_call" | custom-call | bytes 4194304 | tf_op jit(solution)/shard_map/pick/pallas_call | solution.py:76
  128.4 81.1 %all-to-all-done.1.right = bf16[16,2,64,1024]{3,2,1,0:T(8,128)(2,1)} async-done(((bf16[16,2,64,1024]{3,2,1,0:T(8,128)(2,1)}), bf16[16,2,64,1024]{3,2,1,0:T(8,128)(2,1)}, u32[]{:S(2)}, u32[]{:S(2)}) %all-to-all-start.1) | async-done | bytes 4194336 | tf_op jit(solution)/shard_map/all_to_all | solution.py:226
  209.5 6.6 %all-to-all-start.2 = ((bf16[16,2,64,512]{3,2,1,0:T(8,128)(2,1)}), bf16[16,2,64,512]{3,2,1,0:T(8,128)(2,1)S(1)}, u32[]{:S(2)}, u32[]{:S(2)}) async-start(bf16[16,2,64,512]{3,2,1,0:T(8,128)(2,1)} %pick.6), calls=%async_computation.2 | async-start | bytes 4194304 | tf_op jit(solution)/shard_map/all_to_all | solution.py:226
  216.0 0.1 collective-permute-start
  216.2 9.7 %pick.7 = bf16[16,2,64,512]{3,2,1,0:T(8,128)(2,1)} custom-call(s32[8,16]{1,0:T(8,128)} %route.1.table, bf16[64,2,64,1024]{3,2,1,0:T(8,128)(2,1)} %node.7), custom_call_target="tpu_custom_call" | custom-call | bytes 4194304 | tf_op jit(solution)/shard_map/pick/pallas_call | solution.py:76
  225.9 36.0 %all-to-all-done.2.right = bf16[16,2,64,512]{3,2,1,0:T(8,128)(2,1)S(1)} async-done(((bf16[16,2,64,512]{3,2,1,0:T(8,128)(2,1)}), bf16[16,2,64,512]{3,2,1,0:T(8,128)(2,1)S(1)}, u32[]{:S(2)}, u32[]{:S(2)}) %all-to-all-start.2) | async-done | bytes 2097184 | tf_op jit(solution)/shard_map/all_to_all | solution.py:226
  261.9 6.4 %all-to-all-start.3 = ((bf16[16,2,64,512]{3,2,1,0:T(8,128)(2,1)}), bf16[16,2,64,512]{3,2,1,0:T(8,128)(2,1)}, u32[]{:S(2)}, u32[]{:S(2)}) async-start(bf16[16,2,64,512]{3,2,1,0:T(8,128)(2,1)} %pick.7), calls=%async_computation.3 | async-start | bytes 4194304 | tf_op jit(solution)/shard_map/all_to_all | solution.py:226
  268.4 0.0 collective-permute-done.other
  268.4 0.0 copy-done.2
  268.4 15.0 %left_pair.1.left = bf16[2,1024,1024]{2,1,0:T(8,128)(2,1)S(1)} custom-call(s32[8,16]{1,0:T(8,128)S(1)} %copy-done.2, s32[1]{0:T(128)} %bitcast.place, bf16[16,2,64,1024]{3,2,1,0:T(8,128)(2,1)} %all-to-all-done.own, bf16[16,2,64,1024]{3,2,1,0:T(8,128)(2,1)} %collective-permute-done.other), custom_call_target="tpu_custom_call" | custom-call | flops 8589934592 | bytes 12582912 | tf_op jit(solution)/shard_map/left_pair/pallas_call | solution.py:140
  283.4 0.0 copy-start.4
  283.4 1.9 copy-done.4
  285.3 12.3 %product.3.left = bf16[2,1024,1024]{2,1,0:T(8,128)(2,1)S(1)} custom-call(bf16[2,1024,1024]{2,1,0:T(8,128)(2,1)} %copy-done.4, bf16[16,2,64,1024]{3,2,1,0:T(8,128)(2,1)} %all-to-all-done.1.right), custom_call_target="tpu_custom_call" | custom-call | flops 8589934592 | bytes 12582912 | tf_op jit(solution)/shard_map/product/pallas_call | solution.py:185
  297.6 0.0 copy-start.3
  297.6 1.9 copy-done.3
  299.6 6.8 %product.4 = bf16[16,2,64,512]{3,2,1,0:T(8,128)(2,1)S(1)} custom-call(bf16[2,1024,1024]{2,1,0:T(8,128)(2,1)} %copy-done.3, bf16[16,2,64,512]{3,2,1,0:T(8,128)(2,1)S(1)} %all-to-all-done.2.right), custom_call_target="tpu_custom_call" | custom-call | flops 4294967296 | bytes 8388608 | tf_op jit(solution)/shard_map/product/pallas_call | solution.py:185
  306.4 0.0 copy-start
  306.4 1.3 copy-done
  307.7 6.5 %all-to-all-done.3.right = bf16[16,2,64,512]{3,2,1,0:T(8,128)(2,1)} async-done(((bf16[16,2,64,512]{3,2,1,0:T(8,128)(2,1)}), bf16[16,2,64,512]{3,2,1,0:T(8,128)(2,1)}, u32[]{:S(2)}, u32[]{:S(2)}) %all-to-all-start.3) | async-done | bytes 2097184 | tf_op jit(solution)/shard_map/all_to_all | solution.py:226
  314.2 6.6 %all-to-all-start.4 = ((bf16[16,2,64,512]{3,2,1,0:T(8,128)(2,1)}), bf16[16,2,64,512]{3,2,1,0:T(8,128)(2,1)S(1)}, u32[]{:S(2)}, u32[]{:S(2)}) async-start(bf16[16,2,64,512]{3,2,1,0:T(8,128)(2,1)} %copy-done), calls=%async_computation.4 | async-start | bytes 4194304 | tf_op jit(solution)/shard_map/all_to_all | solution.py:226
  320.8 7.4 %product.5 = bf16[16,2,64,512]{3,2,1,0:T(8,128)(2,1)S(1)} custom-call(bf16[2,1024,1024]{2,1,0:T(8,128)(2,1)} %copy-done.3, bf16[16,2,64,512]{3,2,1,0:T(8,128)(2,1)} %all-to-all-done.3.right), custom_call_target="tpu_custom_call" | custom-call | flops 4294967296 | bytes 8388608 | tf_op jit(solution)/shard_map/product/pallas_call | solution.py:185
  328.2 1.3 copy-done.1
  329.5 37.2 %all-to-all-done.4.refs_0_ = bf16[16,2,64,512]{3,2,1,0:T(8,128)(2,1)S(1)} async-done(((bf16[16,2,64,512]{3,2,1,0:T(8,128)(2,1)}), bf16[16,2,64,512]{3,2,1,0:T(8,128)(2,1)S(1)}, u32[]{:S(2)}, u32[]{:S(2)}) %all-to-all-start.4) | async-done | bytes 2097184 | tf_op jit(solution)/shard_map/all_to_all | solution.py:226
  366.7 53.8 %all_to_all.30.refs_1_ = bf16[16,2,64,512]{3,2,1,0:T(8,128)(2,1)S(1)} all-to-all(bf16[16,2,64,512]{3,2,1,0:T(8,128)(2,1)} %copy-done.1), channel_id=1, replica_groups=mesh['grp'=2,'node'=16] {'node'}, dimensions={0} | all-to-all | bytes 4194304 | tf_op jit(solution)/shard_map/all_to_all | solution.py:226
  420.5 3.8 diagrams.1
  (2 shorter events, 0.0 us)
Async XLA Ops:
  15.0 97.1 %all-to-all-start = ((bf16[16,2,64,1024]{3,2,1,0:T(8,128)(2,1)}), bf16[16,2,64,1024]{3,2,1,0:T(8,128)(2,1)}, u32[]{:S(2)}, u32[]{:S(2)}) async-start(bf16[16,2,64,1024]{3,2,1,0:T(8,128)(2,1)} %pick.4), calls=%async_computation | async-start | bytes 8388608 | tf_op jit(solution)/shard_map/all_to_all | solution.py:226
  112.1 97.4 %all-to-all-start.1 = ((bf16[16,2,64,1024]{3,2,1,0:T(8,128)(2,1)}), bf16[16,2,64,1024]{3,2,1,0:T(8,128)(2,1)}, u32[]{:S(2)}, u32[]{:S(2)}) async-start(bf16[16,2,64,1024]{3,2,1,0:T(8,128)(2,1)} %pick.5), calls=%async_computation.1 | async-start | bytes 8388608 | tf_op jit(solution)/shard_map/all_to_all | solution.py:226
  209.5 52.4 %all-to-all-start.2 = ((bf16[16,2,64,512]{3,2,1,0:T(8,128)(2,1)}), bf16[16,2,64,512]{3,2,1,0:T(8,128)(2,1)S(1)}, u32[]{:S(2)}, u32[]{:S(2)}) async-start(bf16[16,2,64,512]{3,2,1,0:T(8,128)(2,1)} %pick.6), calls=%async_computation.2 | async-start | bytes 4194304 | tf_op jit(solution)/shard_map/all_to_all | solution.py:226
  216.0 52.3 %collective-permute-start = (bf16[16,2,64,1024]{3,2,1,0:T(8,128)(2,1)}, bf16[16,2,64,1024]{3,2,1,0:T(8,128)(2,1)}, u32[]{:S(2)}, u32[]{:S(2)}) collective-permute-start(bf16[16,2,64,1024]{3,2,1,0:T(8,128)(2,1)} %all-to-all-done.own), channel_id=1, source_target_pairs={{0,1},{1,0},{2,3},{3,2},{4,5},{5,4},{6,7},{7,6},{8,9},{9,8},{10,11... | collective-permute-start | bytes 12582920 | tf_op jit(solution)/shard_map/ppermute | solution.py:239
  225.9 42.5 %copy-start.2 = (s32[8,16]{1,0:T(8,128)S(1)}, s32[8,16]{1,0:T(8,128)}, u32[]{:S(2)}) copy-start(s32[8,16]{1,0:T(8,128)} %route.1.table) | copy-start | bytes 1540
  261.9 52.3 %all-to-all-start.3 = ((bf16[16,2,64,512]{3,2,1,0:T(8,128)(2,1)}), bf16[16,2,64,512]{3,2,1,0:T(8,128)(2,1)}, u32[]{:S(2)}, u32[]{:S(2)}) async-start(bf16[16,2,64,512]{3,2,1,0:T(8,128)(2,1)} %pick.7), calls=%async_computation.3 | async-start | bytes 4194304 | tf_op jit(solution)/shard_map/all_to_all | solution.py:226
  283.4 2.0 copy-start.4
  297.6 2.0 copy-start.3
  306.4 1.3 copy-start
  314.2 52.4 %all-to-all-start.4 = ((bf16[16,2,64,512]{3,2,1,0:T(8,128)(2,1)}), bf16[16,2,64,512]{3,2,1,0:T(8,128)(2,1)S(1)}, u32[]{:S(2)}, u32[]{:S(2)}) async-start(bf16[16,2,64,512]{3,2,1,0:T(8,128)(2,1)} %copy-done), calls=%async_computation.4 | async-start | bytes 4194304 | tf_op jit(solution)/shard_map/all_to_all | solution.py:226
  328.2 1.3 copy-start.1
